TPU v7x, 32 devices: a whole 2x2x4 slice. The times are simulated.
32 devices in a mesh: blk: 16 (over z, y, x), aux: 2 (over core).
Axes of the slice: x: 2, y: 2, z: 4, core: 2. Of those that a mesh axis runs over, the one named last changes fastest.
Arguments:
- three_centre: bfloat16 [2048, 4, 4096], P('blk', 'aux'), may hold values from -6 to 6
- occupied_blocks: bfloat16 [128, 64, 64], P('blk'), may hold values from -1.5 to 1.5
- virtual_blocks: bfloat16 [128, 64, 64], P('blk'), may hold values from -1.5 to 1.5
- row_slot: int32 [2048], P('blk'), may hold values from 0 to 7
- col_slot: int32 [2048], P('blk'), may hold values from 0 to 7
- block_owner: int32 [2048, 1], P('blk'), may hold values from 0 to 15; in each aligned block of 128 rows (0 to 127, 128 to 255, ...) at most 16 rows name the same one
Outputs:
- polarizability: float32 [128, 4, 4], P('blk', 'aux')
Inputs may be any that keep to these rules, and one draw needn't show every extreme that they name: `block_owner`: among the 128 blocks stored on one index of blk, no owner is named more than 16 times, a bound that some block reaches.
All inputs are finite; a program needn't handle non-finite values.
Results may differ from a plain program's by a relative error of at most 0.0003.
Values may be sent and summed in bfloat16 or wider, within the bound.
No kernel may reach another device: no remote copies, remote signals or barrier semaphores. Data moves between devices by JAX's collectives and lax.ppermute only.
A program may use at most 64 MiB of HBM per device.

v0:
```python
import jax
import jax.numpy as jnp
from jax import lax
from jax.sharding import PartitionSpec as P


def pair_up(values, scale):
    whole = lax.all_gather(values, "aux", axis=1, tiled=True)
    return jnp.einsum("ipc,iqc->ipq", values, whole, preferred_element_type=jnp.float32) * scale


def body(three_centre, occupied_blocks, virtual_blocks, row_slot, col_slot, block_owner):
    block_count, aux_local, width = three_centre.shape
    groups_dev = occupied_blocks.shape[0]
    group_size = occupied_blocks.shape[1]
    scale = 0.25 / (group_size * group_size)
    group_range = jnp.arange(groups_dev, dtype=jnp.int32)
    row_pick = (row_slot[:, None] == group_range[None, :]).astype(jnp.bfloat16)
    occ_pick = jnp.einsum(
        "kg,gml->kml", row_pick, occupied_blocks, preferred_element_type=jnp.float32
    ).astype(jnp.bfloat16)
    blocks = three_centre.reshape(block_count, aux_local, group_size, group_size)
    half_done = jnp.einsum(
        "kpmn,kml->kpln", blocks, occ_pick, preferred_element_type=jnp.float32
    ).astype(jnp.bfloat16)
    owner = block_owner[:, 0]
    every_virt = lax.all_gather(virtual_blocks, "blk", axis=0, tiled=True)
    column = owner * groups_dev + col_slot
    virt_pick = every_virt[column]
    finished = jnp.einsum(
        "kpln,knv->kplv", half_done, virt_pick, preferred_element_type=jnp.float32
    ).astype(jnp.bfloat16)
    products = pair_up(finished.reshape(block_count, aux_local, width), scale)
    pick = (
        column[:, None] == jnp.arange(groups_dev * lax.axis_size("blk"), dtype=jnp.int32)[None, :]
    ).astype(jnp.float32)
    return lax.psum_scatter(
        jnp.einsum("kg,kpq->gpq", pick, products, precision=lax.Precision.HIGHEST),
        "blk",
        scatter_dimension=0,
        tiled=True,
    )


def solution(mesh):
    in_specs = (
        P("blk", "aux", None),
        P("blk", None, None),
        P("blk", None, None),
        P("blk"),
        P("blk"),
        P("blk", None),
    )
    out_specs = P("blk", "aux", None)
    return jax.shard_map(body, mesh=mesh, in_specs=in_specs, out_specs=out_specs, check_vma=False)
```

profile of v0, /device:TPU:0, one launch (start us, length us, event | category | flops | bytes accessed | tf_op | source)
XLA Modules:
  0.0 163.8 jit_solution(4122768177600939639)
XLA Ops:
  6.5 0.0 copy-start
  6.5 0.0 all-gather.3.cloned.1.call-start
  6.5 0.7 all-gather.3.cloned.1.call-update
  7.3 0.0 all-gather.5.cloned.1.call-start
  7.3 4.9 %copy.10 = bf16[128,2,4096]{0,2,1:T(8,128)(2,1)S(1)} copy(bf16[128,2,4096]{2,1,0:T(2,128)(2,1)} %param.6) | data formatting | bytes 4194304 | tf_op args[0]
  12.2 0.0 copy-start.1
  12.2 6.5 %copy.12 = bf16[128,2,64,64]{3,2,1,0:T(8,128)(2,1)} copy(bf16[128,2,64,64]{0,3,2,1:T(8,128)(2,1)S(1)} %bitcast.31) | data formatting | bytes 4194304 | tf_op jit(solution)/shard_map/reshape | solution.py:22
  18.7 0.0 copy-done
  18.7 0.0 copy-done.1
  18.7 0.0 copy-start.2
  18.7 0.0 copy-start.3
  18.7 0.5 fusion.11
  19.3 3.5 %copy.18 = bf16[128,64,64,1]{1,2,3,0:T(8,128)(2,1)S(1)} copy(bf16[128,64,64,1]{0,2,1,3:T(8,128)(2,1)S(1)} %fusion.11) | data formatting | bytes 2097152 | tf_op jit(solution)/shard_map/convert_element_type | solution.py:21
  22.8 0.0 copy-done.2
  22.8 0.0 copy-done.3
  22.8 50.8 %all-gather.3.cloned.1.call-done = bf16[128,64,64]{2,1,0:T(8,128)(2,1)} async-done(((bf16[8,64,64]{2,1,0:T(8,128)(2,1)}), bf16[128,64,64]{2,1,0:T(8,128)(2,1)}) %all-gather.3.cloned.1.call-update) | async-done | bytes 1048592 | tf_op jit(solution)/shard_map/all_gather | solution.py:27
  73.6 3.8 %gather_fusion = bf16[128,64,64]{2,1,0:T(8,128)(2,1)} fusion(bf16[128,64,64]{2,1,0:T(8,128)(2,1)} %all-gather.3.cloned.1.call-done, s32[1024]{0:T(1024)S(1)} %pad_clamp_fusion), kind=kCustom, calls=%fused_computation | custom fusion | bytes 2097664 | tf_op jit(solution)/shard_map/gather | solution.py:29
  77.3 7.2 %fusion.7 = bf16[128,2,64,64]{3,2,1,0:T(8,128)(2,1)} fusion(bf16[128,64,64,1]{1,2,3,0:T(8,128)(2,1)S(1)} %copy.18, bf16[128,2,64,64]{3,2,1,0:T(8,128)(2,1)} %copy.12, bf16[128,64,64]{2,1,0:T(8,128)(2,1)} %gather_fusion), kind=kOutput, calls=%fused_computation.7 | convolution fusion | flops 270532608 | bytes 6291456 | tf_op jit(solution)/shard_map/kpln,knv->kplv/dot_general | solution.py:30
  84.5 5.6 %copy.13 = bf16[128,2,64,64]{0,3,2,1:T(8,128)(2,1)S(1)} copy(bf16[128,2,64,64]{3,2,1,0:T(8,128)(2,1)} %fusion.7) | data formatting | bytes 4194304 | tf_op jit(solution)/shard_map/convert_element_type | solution.py:32
  90.2 2.9 %copy.14 = bf16[128,2,4096]{2,0,1:T(8,128)(2,1)} copy(bf16[128,2,4096]{0,2,1:T(8,128)(2,1)S(1)} %bitcast.29) | data formatting | bytes 4194304 | tf_op jit(solution)/shard_map/reshape | solution.py:33
  93.0 0.0 copy-start.4
  93.0 0.0 all-gather.5.cloned.1.call-update
  93.1 0.6 copy-done.4
  93.7 0.6 dynamic-slice
  94.9 4.0 %copy.15 = bf16[128,2,4096]{2,1,0:T(2,128)(2,1)} copy(bf16[128,2,4096]{0,2,1:T(8,128)(2,1)S(1)} %bitcast.30) | data formatting | bytes 4194304 | tf_op jit(solution)/shard_map/reshape | solution.py:33
  98.9 6.6 %all-gather.5.cloned.1.call-done = bf16[128,4,4096]{2,0,1:T(8,128)(2,1)} async-done(((bf16[128,2,4096]{2,0,1:T(8,128)(2,1)}), bf16[128,4,4096]{2,0,1:T(8,128)(2,1)}) %all-gather.5.cloned.1.call-update) | async-done | bytes 4194320 | tf_op jit(solution)/shard_map/all_gather | solution.py:8
  105.5 8.6 %fusion.12 = f32[128,2,4]{2,1,0:T(2,128)S(1)} fusion(bf16[128,2,4096]{2,1,0:T(2,128)(2,1)} %copy.15, bf16[128,4,4096]{2,0,1:T(8,128)(2,1)} %all-gather.5.cloned.1.call-done), kind=kOutput, calls=%fused_computation.11 | convolution fusion | flops 8389632 | bytes 6295552 | tf_op jit(solution)/shard_map/ipc,iqc->ipq/dot_general | solution.py:9
  114.1 0.1 copy.17
  114.2 0.2 fusion.16
  114.4 42.0 %all-reduce = f32[128,2,4]{0,2,1:T(4,128)S(1)} all-reduce(f32[128,2,4]{0,2,1:T(4,128)S(1)} %bitcast.33), channel_id=2, replica_groups=mesh['blk'=16,'aux'=2] {'blk'}, use_global_device_ids=true, to_apply=%region_0.0.clone | all-reduce | flops 1024 | bytes 8192
  156.3 0.7 constant_dynamic-slice_fusion
  (2 shorter events, 0.0 us)
Async XLA Ops:
  6.5 12.2 %copy-start = (bf16[8,64,64]{2,1,0:T(8,128)(2,1)S(1)}, bf16[8,64,64]{2,1,0:T(8,128)(2,1)}, u32[]{:S(2)}) copy-start(bf16[8,64,64]{2,1,0:T(8,128)(2,1)} %param.7) | copy-start | bytes 196612
  6.5 67.0 %all-gather.3.cloned.1.call-start = ((), (), s32[]{:S(2)}) async-start(), calls=%async_computation | async-start | bytes 2228224 | tf_op jit(solution)/shard_map/all_gather | solution.py:27
  7.3 98.3 %all-gather.5.cloned.1.call-start = ((), (), s32[]{:S(2)}) async-start(), calls=%async_computation.1 | async-start | bytes 6291456 | tf_op jit(solution)/shard_map/all_gather | solution.py:8
  12.2 6.5 %copy-start.1 = (s32[128]{0:T(128)S(1)}, s32[128]{0:T(128)}, u32[]{:S(2)}) copy-start(s32[128]{0:T(128)} %param.9) | copy-start | bytes 1540
  18.7 4.1 %copy-start.2 = (s32[128]{0:T(128)S(1)}, s32[128]{0:T(128)}, u32[]{:S(2)}) copy-start(s32[128]{0:T(128)} %param.10) | copy-start | bytes 1540
  18.7 4.1 %copy-start.3 = (s32[128,1]{0,1:T(1,128)S(1)}, s32[128,1]{0,1:T(1,128)}, u32[]{:S(2)}) copy-start(s32[128,1]{0,1:T(1,128)} %param.11) | copy-start | bytes 1540
  93.0 0.7 copy-start.4
Sparse Core Ops, SparseCore 0:
  10.1 63.3 all-gather.2
  93.2 12.2 all-gather.4
where the time goes:
time: 164 us
  waiting for transfers between devices  58.1 us (35%)
  blocking collectives  42 us (26%)
  local copies, waits for them, and re-layouts  33.1 us (20%)
  matrix products  16.5 us (10%)
  between operations  14.1 us (9%)
    all_gather x1, waiting for transfers between devices, body(): every_virt = lax.all_gather(virtual_blocks, 'blk', axis=0, tiled=True)  50.8 us
    unnamed x1, blocking collectives  42 us
    dot_general x1, matrix products, pair_up(): jnp.einsum('ipc,iqc->ipq', values, whole, preferred_element_type=jnp.floa...  8.55 us
    dot_general x1, matrix products, body(): jnp.einsum('kpln,knv->kplv', half_done, virt_pick, preferred_element_type...  7.18 us
    reshape x2, local copies, waits for them, and re-layouts, body(): products = pair_up(finished.reshape(block_count, aux_local, width), scale)  6.81 us
    unnamed x13, local copies, waits for them, and re-layouts  6.78 us
    all_gather x1, waiting for transfers between devices, pair_up(): whole = lax.all_gather(values, 'aux', axis=1, tiled=True)  6.64 us
    reshape x1, local copies, waits for them, and re-layouts, body(): three_centre.reshape(block_count, aux_local, group_size, group_size)  6.48 us
  transfers between devices with their start and end apart: 2, of which 2 were waited for; matrix products, arithmetic and copies ran while one was open for 12% of the time, Pallas kernels for 0%

commit v1 on v0

v1 whole, which is shorter than its diff:
```python
import functools

import jax
import jax.numpy as jnp
from jax import lax
from jax.experimental import pallas as pl
from jax.experimental.pallas import tpu as pltpu
from jax.sharding import PartitionSpec as P

F32 = jnp.float32
BF16 = jnp.bfloat16
SMEM = pl.BlockSpec(memory_space=pltpu.SMEM)
VMEM = pl.BlockSpec(memory_space=pltpu.VMEM)


def rounds_of(count):
    bits = count.bit_length() - 1
    found = []
    while bits:
        low = (bits - 1) // 2 * 2
        found.append([step << low for step in range(1, 1 << (bits - low))])
        bits = low
    return found


def flip(values, distance, count):
    return lax.ppermute(values, "blk", [(i, i ^ distance) for i in range(count)])


def swap_cores(values):
    return lax.ppermute(values, "aux", [(0, 1), (1, 0)])


def half_kernel(row_slot, blocks_ref, occ_ref, keep_ref, send_ref, expand_ref):
    groups, size, _ = occ_ref.shape
    wide = 2 * size
    core = lax.axis_index("aux")
    row = lax.broadcasted_iota(jnp.int32, (size, wide), 1)
    mu = lax.broadcasted_iota(jnp.int32, (size, wide), 0)
    order = jnp.where(mu == (row % size) // 2 * 2 + row // size, 1.0, 0.0).astype(BF16)
    left = lax.broadcasted_iota(jnp.int32, (wide, wide), 0) // size
    same = left == lax.broadcasted_iota(jnp.int32, (wide, wide), 1) % 2
    for group in range(groups):
        occ = occ_ref[group]
        twice = jnp.concatenate([occ, occ], axis=1)
        spread = lax.dot_general(twice, order, (((0,), (0,)), ((), ())), preferred_element_type=F32)
        expand_ref[group] = jnp.where(same, spread, 0.0).astype(BF16)
    pairs = keep_ref.shape[0]
    near = lax.broadcasted_iota(jnp.int32, (size, wide), 1) < size
    near_out = lax.broadcasted_iota(jnp.int32, (wide, wide), 1) < size

    def one(first, out_ref, index):
        block = 2 * (first + index)
        one_block, two_block = blocks_ref[block], blocks_ref[block + 1]
        one_turned = jnp.concatenate([one_block[:, size:], one_block[:, :size]], axis=1)
        two_turned = jnp.concatenate([two_block[:, size:], two_block[:, :size]], axis=1)
        stacked = jnp.concatenate(
            [jnp.where(near, one_block, two_turned), jnp.where(near, one_turned, two_block)], axis=0
        )
        one_out = jnp.dot(expand_ref[row_slot[block]], stacked, preferred_element_type=F32)
        two_out = jnp.dot(expand_ref[row_slot[block + 1]], stacked, preferred_element_type=F32)
        out_ref[index] = jnp.where(near_out, one_out, two_out).astype(BF16)

    @pl.loop(0, pairs, unroll=4)
    def _(index):
        one((1 - core) * pairs, send_ref, index)

    @pl.loop(0, pairs, unroll=4)
    def _(index):
        one(core * pairs, keep_ref, index)


def chi_kernel(
    count, groups_dev, scale, col_slot, owner, own_ref, other_ref, near_virt, far_virt, out_ref
):
    pairs, wide, _ = own_ref.shape
    size = wide // 2
    core = lax.axis_index("aux")
    me = lax.axis_index("blk")
    half_groups = groups_dev // 2
    groups = count * groups_dev
    lane = lax.broadcasted_iota(jnp.int32, (size, wide), 1)
    low = lane < size
    group_range = lax.broadcasted_iota(jnp.int32, (wide, groups), 1)
    upper = lax.broadcasted_iota(jnp.int32, (wide, groups), 0) < size

    def virt_of(block, keep):
        slot, place = col_slot[block], owner[block] ^ me
        tile = (slot % half_groups) // 2
        is_far = slot // half_groups != core
        found = jnp.where(is_far, far_virt[place, tile], near_virt[place, tile])
        turned = jnp.concatenate([found[:, size:], found[:, :size]], axis=1)
        wanted = jnp.where((slot % 2 == 1) == keep, found, turned)
        mine = (lane >= size) == keep
        return jnp.where(mine, wanted, jnp.zeros_like(wanted))

    def one(index, total):
        block = 2 * (core * pairs + index)
        virt = jnp.concatenate([virt_of(block, False), virt_of(block + 1, True)], axis=0)
        full = []
        for ref in (own_ref, other_ref):
            made = jnp.dot(ref[index], virt, preferred_element_type=F32).astype(BF16).astype(F32)
            full += [made[:size], made[size:]]
        sums = {}
        for p in range(4):
            for q in range(p, 4):
                sums[p, q] = sums[q, p] = jnp.sum(full[p] * full[q], axis=0, keepdims=True)
        rows = [sums[p, q] for p in range(2) for q in range(4)]
        rows += [sums[p, q ^ 2] for p in range(2, 4) for q in range(4)]
        values = jnp.concatenate(rows, axis=0)
        first = values.astype(BF16)
        rest = values - first.astype(F32)
        second = rest.astype(BF16)
        third = (rest - second.astype(F32)).astype(BF16)
        parts = jnp.concatenate([first, second, third], axis=0)
        one_column = owner[block] * groups_dev + col_slot[block]
        two_column = owner[block + 1] * groups_dev + col_slot[block + 1]
        pick = jnp.where(group_range == jnp.where(upper, one_column, two_column), 1.0, 0.0).astype(BF16)
        return total + jnp.dot(parts, pick, preferred_element_type=F32)

    total = lax.fori_loop(0, pairs, one, jnp.zeros((48, groups), F32), unroll=4)
    summed = (total[:16] + total[16:32] + total[32:]) * scale
    for start in range(0, groups, wide):
        square = jnp.concatenate([summed[:, start:start + wide], jnp.zeros((wide - 16, wide), F32)], axis=0)
        out_ref[start:start + wide, :] = square.T


def body(count, three_centre, occupied_blocks, virtual_blocks, row_slot, col_slot, block_owner):
    block_count, aux_local, width = three_centre.shape
    groups_dev, size, _ = occupied_blocks.shape
    scale = 0.25 / (size * size)
    wide = 2 * size
    pairs = block_count // 4
    core = lax.axis_index("aux")
    me = lax.axis_index("blk")
    rounds = rounds_of(count)

    quarter = lax.dynamic_slice_in_dim(virtual_blocks, core * (groups_dev // 2), groups_dev // 2)
    near_virt = jnp.concatenate([quarter[0::2], quarter[1::2]], axis=2)[None]
    blocks = three_centre.reshape(block_count, aux_local, width // wide, wide)
    blocks = blocks.transpose(0, 2, 1, 3).reshape(block_count, size, wide)
    keep, send = pl.pallas_call(
        half_kernel,
        out_shape=[jax.ShapeDtypeStruct((pairs, wide, wide), BF16)] * 2,
        in_specs=[SMEM, VMEM, VMEM],
        out_specs=[VMEM, VMEM],
        scratch_shapes=[pltpu.VMEM((groups_dev, wide, wide), BF16)],
        compiler_params=pltpu.CompilerParams(vmem_limit_bytes=32 * 1024 * 1024),
        cost_estimate=pl.CostEstimate(flops=10**9, bytes_accessed=4 * 1024 * 1024, transcendentals=0),
        name="half",
    )(row_slot, blocks, occupied_blocks)
    other = swap_cores(send)
    for distances in rounds:
        step = distances[0]
        arrived = [near_virt] + [flip(near_virt, distance, count) for distance in distances]
        near_virt = jnp.stack(arrived, axis=1).reshape((-1,) + near_virt.shape[1:])
    far_virt = swap_cores(near_virt)

    partial = pl.pallas_call(
        functools.partial(chi_kernel, count, groups_dev, scale),
        out_shape=jax.ShapeDtypeStruct((count * groups_dev, wide), F32),
        in_specs=[SMEM, SMEM, VMEM, VMEM, VMEM, VMEM],
        out_specs=VMEM,
        compiler_params=pltpu.CompilerParams(vmem_limit_bytes=48 * 1024 * 1024),
        cost_estimate=pl.CostEstimate(flops=10**9, bytes_accessed=4 * 1024 * 1024, transcendentals=0),
        name="chi",
    )(col_slot, block_owner.reshape(block_count), keep, other, near_virt, far_virt)

    partial = partial.reshape(count, groups_dev, wide)
    for distances in rounds:
        parts = len(distances) + 1
        split = partial.reshape(parts, -1, groups_dev, wide)
        mine = me // distances[0] % parts
        partial = lax.dynamic_index_in_dim(split, mine, 0, False)
        for turn, distance in enumerate(distances):
            leaving = lax.dynamic_index_in_dim(split, mine ^ (turn + 1), 0, False)
            partial = partial + flip(leaving, distance, count)
    partial = partial[0]
    theirs = swap_cores(partial[:, :16])
    both = (partial[:, :8] + theirs[:, 8:16]).reshape(groups_dev, 2, 2, 2)
    return jnp.where(core == 0, both, both[:, :, ::-1]).reshape(groups_dev, 2, 4)


def solution(mesh):
    in_specs = (
        P("blk", "aux", None),
        P("blk", None, None),
        P("blk", None, None),
        P("blk"),
        P("blk"),
        P("blk", None),
    )
    out_specs = P("blk", "aux", None)
    return jax.shard_map(
        functools.partial(body, mesh.shape["blk"]),
        mesh=mesh,
        in_specs=in_specs,
        out_specs=out_specs,
        check_vma=False,
    )
```

time: 164 us -> 73.4 us (0.45)
  blocking collectives: 42 us -> 0 us
  local copies, waits for them, and re-layouts: 33.1 us -> 6 us
  waiting for transfers between devices: 58.1 us -> 36.3 us
  starting transfers between devices: 0.04 us -> 17.6 us
  matrix products: 16.5 us -> 0 us
  between operations: 14.1 us -> 0.23 us
  Pallas kernels: 0 us -> 12.2 us
    all_gather x2 -> x0, waiting for transfers between devices: 57.4 us -> none  [the longest x1 50.8 us: body(): every_virt = lax.all_gather(virtual_blocks, 'blk', axis=0, tiled=True)]
    unnamed x1 -> x0, blocking collectives: 42 us -> none
    ppermute x0 -> x15, waiting for transfers between devices: none -> 36.3 us  [the longest x12 33.3 us: flip(): lax.ppermute(values, 'blk', [(i, i ^ distance) for i in range(count)])]
    ppermute x0 -> x15, starting transfers between devices: none -> 17.6 us  [the longest x12 17 us: flip(): lax.ppermute(values, 'blk', [(i, i ^ distance) for i in range(count)])]
    dot_general x3 -> x0, matrix products: 16.3 us -> none  [the longest x1 8.55 us: pair_up(): jnp.einsum('ipc,iqc->ipq', values, whole, preferred_element_type=jnp.floa...]
    reshape x3 -> x0, local copies, waits for them, and re-layouts: 13.3 us -> none  [the longest x2 6.81 us: body(): products = pair_up(finished.reshape(block_count, aux_local, width), scale)]
    pallas_call x0 -> x2, Pallas kernels: none -> 12.2 us  [the longest x1 6.68 us: body(): pl.pallas_call(functools.partial(chi_kernel, count, groups_dev, scale), o...]
    convert_element_type x2 -> x0, local copies, waits for them, and re-layouts: 9.14 us -> none  [the longest x1 5.64 us: body(): finished = jnp.einsum('kpln,knv->kplv', half_done, virt_pick, preferred_e...]
  transfers between devices with their start and end apart: 2 -> 15, of which waited for: 2 -> 12; matrix products, arithmetic and copies ran while one was open for 12% -> 1% of each run, Pallas kernels for 0% -> 0%
where the time goes in v1:
time: 73.4 us; the launch traced here: 73.2 us
  waiting for transfers between devices  36.3 us (49%)
  starting transfers between devices  17.6 us (24%)
  Pallas kernels  12.2 us (17%)
  local copies, waits for them, and re-layouts  6 us (8%)
  other arithmetic  0.85 us (1%)
    ppermute x12, waiting for transfers between devices, flip(): lax.ppermute(values, 'blk', [(i, i ^ distance) for i in range(count)])  33.3 us
    ppermute x12, starting transfers between devices, flip(): lax.ppermute(values, 'blk', [(i, i ^ distance) for i in range(count)])  17 us
    pallas_call x1, Pallas kernels, body(): pl.pallas_call(functools.partial(chi_kernel, count, groups_dev, scale), o...  6.68 us
    pallas_call x1, Pallas kernels, body(): pl.pallas_call(half_kernel, out_shape=[jax.ShapeDtypeStruct((pairs, wide,...  5.55 us
    unnamed x16, local copies, waits for them, and re-layouts  5.42 us
    ppermute x3, waiting for transfers between devices, swap_cores(): return lax.ppermute(values, 'aux', [(0, 1), (1, 0)])  3 us
  transfers between devices with their start and end apart: 15, of which 12 were waited for; matrix products, arithmetic and copies ran while one was open for 1% of the time, Pallas kernels for 0%

profile of v1, /device:TPU:0, one launch (start us, length us, event | category | flops | bytes accessed | tf_op | source)
XLA Modules:
  0.0 73.2 jit_solution(951908498211643790)
XLA Ops:
  0.0 0.0 copy-start
  0.0 1.6 %copy-done.1 = bf16[128,2,4096]{2,1,0:T(2,128)(2,1)S(1)} copy-done((bf16[128,2,4096]{2,1,0:T(2,128)(2,1)S(1)}, bf16[128,2,4096]{2,1,0:T(2,128)(2,1)}, u32[]{:S(2)}) %copy-start.1) | copy-done | bytes 2097176
  1.6 0.9 %copy-done.2 = bf16[8,64,64]{2,1,0:T(8,128)(2,1)S(1)} copy-done((bf16[8,64,64]{2,1,0:T(8,128)(2,1)S(1)}, bf16[8,64,64]{2,1,0:T(8,128)(2,1)}, u32[]{:S(2)}) %copy-start.2) | copy-done | bytes 65560
  2.5 0.7 copy-done.3
  3.2 5.5 %half.1 = (bf16[32,128,128]{2,1,0:T(8,128)(2,1)S(1)}, bf16[32,128,128]{2,1,0:T(8,128)(2,1)S(1)}) custom-call(s32[128]{0:T(128)S(1)} %copy-done.3, bf16[128,64,128]{2,1,0:T(8,128)(2,1)S(1)} %bitcast.38, bf16[8,64,64]{2,1,0:T(8,128)(2,1)S(1)} %copy-done.2), custom_call_target="tpu_custom_call" | custom-call | flops 1000000000 | bytes 4194304 | tf_op jit(solution)/shard_map/half/pallas_call | solution.py:142
  8.7 0.0 copy-start.6
  8.8 1.0 %copy-done.6 = bf16[32,128,128]{2,1,0:T(8,128)(2,1)} copy-done((bf16[32,128,128]{2,1,0:T(8,128)(2,1)}, bf16[32,128,128]{2,1,0:T(8,128)(2,1)S(1)}, u32[]{:S(2)}) %copy-start.6) | copy-done | bytes 1048600
  9.8 0.5 collective-permute-start
  10.2 0.1 fusion.5
  10.3 4.7 %collective-permute-start.3 = (bf16[1,2,64,128]{3,2,1,0:T(8,128)(2,1)S(1)}, bf16[1,2,64,128]{3,2,1,0:T(8,128)(2,1)S(1)}, u32[]{:S(2)}, u32[]{:S(2)}) collective-permute-start(bf16[1,2,64,128]{3,2,1,0:T(8,128)(2,1)S(1)} %get-tuple-element.19), channel_id=1, source_target_pairs={{0,24},{2,26},{4,28},{6,30},{8,16},{10,18},{12,20},{14,22},{16,8},... | collective-permute-start | bytes 98312 | tf_op jit(solution)/shard_map/ppermute | solution.py:27
  15.0 0.0 collective-permute-start.2
  15.0 0.6 collective-permute-start.1
  15.6 1.4 %collective-permute-done.3 = bf16[1,2,64,128]{3,2,1,0:T(8,128)(2,1)S(1)} collective-permute-done((bf16[1,2,64,128]{3,2,1,0:T(8,128)(2,1)S(1)}, bf16[1,2,64,128]{3,2,1,0:T(8,128)(2,1)S(1)}, u32[]{:S(2)}, u32[]{:S(2)}) %collective-permute-start.3) | collective-permute-done | bytes 32800 | tf_op jit(solution)/shard_map/ppermute | solution.py:27
  17.1 2.8 %collective-permute-done.2 = bf16[1,2,64,128]{3,2,1,0:T(8,128)(2,1)S(1)} collective-permute-done((bf16[1,2,64,128]{3,2,1,0:T(8,128)(2,1)S(1)}, bf16[1,2,64,128]{3,2,1,0:T(8,128)(2,1)S(1)}, u32[]{:S(2)}, u32[]{:S(2)}) %collective-permute-start.2) | collective-permute-done | bytes 32800 | tf_op jit(solution)/shard_map/ppermute | solution.py:27
  19.8 0.0 collective-permute-done.1
  19.9 2.5 %collective-permute-start.6 = (bf16[4,2,64,128]{3,2,1,0:T(8,128)(2,1)S(1)}, bf16[4,2,64,128]{3,2,1,0:T(8,128)(2,1)S(1)}, u32[]{:S(2)}, u32[]{:S(2)}) collective-permute-start(bf16[4,2,64,128]{3,2,1,0:T(8,128)(2,1)S(1)} %get-tuple-element.13), channel_id=1, source_target_pairs={{0,6},{2,4},{4,2},{6,0},{8,14},{10,12},{12,10},{14,8},{16,22},{18,... | collective-permute-start | bytes 393224 | tf_op jit(solution)/shard_map/ppermute | solution.py:27
  22.4 0.5 collective-permute-start.5
  22.9 0.5 collective-permute-start.4
  23.4 3.1 %collective-permute-done.6 = bf16[4,2,64,128]{3,2,1,0:T(8,128)(2,1)S(1)} collective-permute-done((bf16[4,2,64,128]{3,2,1,0:T(8,128)(2,1)S(1)}, bf16[4,2,64,128]{3,2,1,0:T(8,128)(2,1)S(1)}, u32[]{:S(2)}, u32[]{:S(2)}) %collective-permute-start.6) | collective-permute-done | bytes 131104 | tf_op jit(solution)/shard_map/ppermute | solution.py:27
  26.5 1.8 %collective-permute-done.5 = bf16[4,2,64,128]{3,2,1,0:T(8,128)(2,1)S(1)} collective-permute-done((bf16[4,2,64,128]{3,2,1,0:T(8,128)(2,1)S(1)}, bf16[4,2,64,128]{3,2,1,0:T(8,128)(2,1)S(1)}, u32[]{:S(2)}, u32[]{:S(2)}) %collective-permute-start.5) | collective-permute-done | bytes 131104 | tf_op jit(solution)/shard_map/ppermute | solution.py:27
  28.3 0.1 collective-permute-done.4
  28.4 0.1 pad_maximum_fusion
  28.5 0.1 collective-permute-start.7
  28.6 1.8 %collective-permute-done.7.far_virt = bf16[16,2,64,128]{3,2,1,0:T(8,128)(2,1)S(1)} collective-permute-done((bf16[16,2,64,128]{3,2,1,0:T(8,128)(2,1)S(1)}, bf16[16,2,64,128]{3,2,1,0:T(8,128)(2,1)S(1)}, u32[]{:S(2)}, u32[]{:S(2)}) %collective-permute-start.7) | collective-permute-done | bytes 524320 | tf_op jit(solution)/shard_map/ppermute | solution.py:31
  30.5 0.0 collective-permute-done.other_ref
  30.5 0.0 copy-done.4
  30.5 1.2 %copy-done.7 = bf16[32,128,128]{2,1,0:T(8,128)(2,1)S(1)} copy-done((bf16[32,128,128]{2,1,0:T(8,128)(2,1)S(1)}, bf16[32,128,128]{2,1,0:T(8,128)(2,1)}, u32[]{:S(2)}) %copy-start.7) | copy-done | bytes 1048600
  31.7 6.7 %chi.1 = f32[128,128]{1,0:T(8,128)S(1)} custom-call(s32[128]{0:T(128)S(1)} %copy-done.4, s32[128]{0:T(128)S(1)} %bitcast.39, bf16[32,128,128]{2,1,0:T(8,128)(2,1)S(1)} %copy-done.7, bf16[32,128,128]{2,1,0:T(8,128)(2,1)S(1)} %collective-permute-done.other_ref, bf16[16,2,64,128]{3,2,1,0:T(8,128)(2,1)S(1)} %bitcast.36, ...), custom_call_target="tpu_custom_call" | custom-call | flops 1000000000 | bytes 4194304 | tf_op jit(solution)/shard_map/chi/pallas_call | solution.py:159
  38.4 0.1 copy.12
  38.6 2.2 %collective-permute-start.10 = (f32[4,8,128]{1,2,0:T(8,128)S(1)}, f32[4,8,128]{1,2,0:T(8,128)S(1)}, u32[]{:S(2)}, u32[]{:S(2)}) collective-permute-start(f32[4,8,128]{1,2,0:T(8,128)S(1)} %bitcast.40), channel_id=1, source_target_pairs={{0,24},{2,26},{4,28},{6,30},{8,16},{10,18},{12,20},{14,22},{16,8},... | collective-permute-start | bytes 49160 | tf_op jit(solution)/shard_map/ppermute | solution.py:27
  40.7 0.1 copy.11
  40.8 0.1 collective-permute-start.9
  40.9 0.1 copy.10
  41.1 2.3 %collective-permute-start.8 = (f32[4,8,128]{1,2,0:T(8,128)S(1)}, f32[4,8,128]{1,2,0:T(8,128)S(1)}, u32[]{:S(2)}, u32[]{:S(2)}) collective-permute-start(f32[4,8,128]{1,2,0:T(8,128)S(1)} %bitcast.42), channel_id=1, source_target_pairs={{0,8},{2,10},{4,12},{6,14},{8,0},{10,2},{12,4},{14,6},{16,24},{18,... | collective-permute-start | bytes 49160 | tf_op jit(solution)/shard_map/ppermute | solution.py:27
  43.4 0.1 copy.9
  43.5 6.2 %collective-permute-done.10 = f32[4,8,128]{1,2,0:T(8,128)S(1)} collective-permute-done((f32[4,8,128]{1,2,0:T(8,128)S(1)}, f32[4,8,128]{1,2,0:T(8,128)S(1)}, u32[]{:S(2)}, u32[]{:S(2)}) %collective-permute-start.10) | collective-permute-done | bytes 16416 | tf_op jit(solution)/shard_map/ppermute | solution.py:27
  49.7 14.2 %collective-permute-done.9 = f32[4,8,128]{1,2,0:T(8,128)S(1)} collective-permute-done((f32[4,8,128]{1,2,0:T(8,128)S(1)}, f32[4,8,128]{1,2,0:T(8,128)S(1)}, u32[]{:S(2)}, u32[]{:S(2)}) %collective-permute-start.9) | collective-permute-done | bytes 16416 | tf_op jit(solution)/shard_map/ppermute | solution.py:27
  63.9 0.0 collective-permute-done.8
  63.9 0.1 fusion.1
  64.0 1.7 %collective-permute-start.13 = (f32[1,8,128]{1,2,0:T(8,128)S(1)}, f32[1,8,128]{1,2,0:T(8,128)S(1)}, u32[]{:S(2)}, u32[]{:S(2)}) collective-permute-start(f32[1,8,128]{1,2,0:T(8,128)S(1)} %get-tuple-element.10), channel_id=1, source_target_pairs={{0,6},{2,4},{4,2},{6,0},{8,14},{10,12},{12,10},{14,8},{16,22},{18,... | collective-permute-start | bytes 12296 | tf_op jit(solution)/shard_map/ppermute | solution.py:27
  65.7 1.4 %collective-permute-start.12 = (f32[1,8,128]{1,2,0:T(8,128)S(1)}, f32[1,8,128]{1,2,0:T(8,128)S(1)}, u32[]{:S(2)}, u32[]{:S(2)}) collective-permute-start(f32[1,8,128]{1,2,0:T(8,128)S(1)} %get-tuple-element.11), channel_id=1, source_target_pairs={{0,4},{2,6},{4,0},{6,2},{8,12},{10,14},{12,8},{14,10},{16,20},{18,... | collective-permute-start | bytes 12296 | tf_op jit(solution)/shard_map/ppermute | solution.py:27
  67.0 0.5 collective-permute-start.11
  67.6 2.4 %collective-permute-done.13 = f32[1,8,128]{1,2,0:T(8,128)S(1)} collective-permute-done((f32[1,8,128]{1,2,0:T(8,128)S(1)}, f32[1,8,128]{1,2,0:T(8,128)S(1)}, u32[]{:S(2)}, u32[]{:S(2)}) %collective-permute-start.13) | collective-permute-done | bytes 4128 | tf_op jit(solution)/shard_map/ppermute | solution.py:27
  69.9 0.4 collective-permute-done.12
  70.3 1.0 %collective-permute-done.11 = f32[1,8,128]{1,2,0:T(8,128)S(1)} collective-permute-done((f32[1,8,128]{1,2,0:T(8,128)S(1)}, f32[1,8,128]{1,2,0:T(8,128)S(1)}, u32[]{:S(2)}, u32[]{:S(2)}) %collective-permute-start.11) | collective-permute-done | bytes 4128 | tf_op jit(solution)/shard_map/ppermute | solution.py:27
  71.3 0.1 collective-permute-start.14
  71.4 1.2 %collective-permute-done.14 = f32[8,16]{0,1:T(8,128)S(1)} collective-permute-done((f32[8,16]{0,1:T(8,128)S(1)}, f32[8,16]{0,1:T(8,128)S(1)}, u32[]{:S(2)}, u32[]{:S(2)}) %collective-permute-start.14) | collective-permute-done | bytes 544 | tf_op jit(solution)/shard_map/ppermute | solution.py:31
  72.6 0.6 reverse_select_fusion
  (17 shorter events, 0.2 us)
Async XLA Ops:
  0.0 10.2 %copy-start = (bf16[8,64,64]{2,1,0:T(8,128)(2,1)S(1)}, bf16[8,64,64]{2,1,0:T(8,128)(2,1)}, u32[]{:S(2)}) copy-start(bf16[8,64,64]{2,1,0:T(8,128)(2,1)} %param.8) | copy-start | bytes 196612
  0.0 1.6 %copy-start.1 = (bf16[128,2,4096]{2,1,0:T(2,128)(2,1)S(1)}, bf16[128,2,4096]{2,1,0:T(2,128)(2,1)}, u32[]{:S(2)}) copy-start(bf16[128,2,4096]{2,1,0:T(2,128)(2,1)} %param.6) | copy-start | bytes 6291460
  1.6 0.9 %copy-start.2 = (bf16[8,64,64]{2,1,0:T(8,128)(2,1)S(1)}, bf16[8,64,64]{2,1,0:T(8,128)(2,1)}, u32[]{:S(2)}) copy-start(bf16[8,64,64]{2,1,0:T(8,128)(2,1)} %occ_ref.1) | copy-start | bytes 196612
  2.5 0.7 copy-start.3
  8.7 1.0 %copy-start.6 = (bf16[32,128,128]{2,1,0:T(8,128)(2,1)}, bf16[32,128,128]{2,1,0:T(8,128)(2,1)S(1)}, u32[]{:S(2)}) copy-start(bf16[32,128,128]{2,1,0:T(8,128)(2,1)S(1)} %get-tuple-element.7.own_ref) | copy-start | bytes 3145732
  9.8 20.7 %copy-start.4 = (s32[128]{0:T(128)S(1)}, s32[128]{0:T(128)}, u32[]{:S(2)}) copy-start(s32[128]{0:T(128)} %col_slot.1) | copy-start | bytes 1540
  9.8 20.7 %copy-start.5 = (s32[128,1]{0,1:T(1,128)S(1)}, s32[128,1]{0,1:T(1,128)}, u32[]{:S(2)}) copy-start(s32[128,1]{0,1:T(1,128)} %param.11) | copy-start | bytes 1540
  9.8 20.7 %collective-permute-start = (bf16[32,128,128]{2,1,0:T(8,128)(2,1)S(1)}, bf16[32,128,128]{2,1,0:T(8,128)(2,1)S(1)}, u32[]{:S(2)}, u32[]{:S(2)}) collective-permute-start(bf16[32,128,128]{2,1,0:T(8,128)(2,1)S(1)} %get-tuple-element.8), channel_id=1, source_target_pairs={{0,1},{1,0},{2,3},{3,2},{4,5},{5,4},{6,7},{7,6},{8,9},{9,8},{10,11... | collective-permute-start | bytes 3145736 | tf_op jit(solution)/shard_map/ppermute | solution.py:31
  10.3 6.7 %collective-permute-start.3 = (bf16[1,2,64,128]{3,2,1,0:T(8,128)(2,1)S(1)}, bf16[1,2,64,128]{3,2,1,0:T(8,128)(2,1)S(1)}, u32[]{:S(2)}, u32[]{:S(2)}) collective-permute-start(bf16[1,2,64,128]{3,2,1,0:T(8,128)(2,1)S(1)} %get-tuple-element.19), channel_id=1, source_target_pairs={{0,24},{2,26},{4,28},{6,30},{8,16},{10,18},{12,20},{14,22},{16,8},... | collective-permute-start | bytes 98312 | tf_op jit(solution)/shard_map/ppermute | solution.py:27
  15.0 4.8 %collective-permute-start.2 = (bf16[1,2,64,128]{3,2,1,0:T(8,128)(2,1)S(1)}, bf16[1,2,64,128]{3,2,1,0:T(8,128)(2,1)S(1)}, u32[]{:S(2)}, u32[]{:S(2)}) collective-permute-start(bf16[1,2,64,128]{3,2,1,0:T(8,128)(2,1)S(1)} %get-tuple-element.19), channel_id=1, source_target_pairs={{0,16},{2,18},{4,20},{6,22},{8,24},{10,26},{12,28},{14,30},{16,0},... | collective-permute-start | bytes 98312 | tf_op jit(solution)/shard_map/ppermute | solution.py:27
  15.0 4.8 %collective-permute-start.1 = (bf16[1,2,64,128]{3,2,1,0:T(8,128)(2,1)S(1)}, bf16[1,2,64,128]{3,2,1,0:T(8,128)(2,1)S(1)}, u32[]{:S(2)}, u32[]{:S(2)}) collective-permute-start(bf16[1,2,64,128]{3,2,1,0:T(8,128)(2,1)S(1)} %get-tuple-element.19), channel_id=1, source_target_pairs={{0,8},{2,10},{4,12},{6,14},{8,0},{10,2},{12,4},{14,6},{16,24},{18,... | collective-permute-start | bytes 98312 | tf_op jit(solution)/shard_map/ppermute | solution.py:27
  19.9 6.6 %collective-permute-start.6 = (bf16[4,2,64,128]{3,2,1,0:T(8,128)(2,1)S(1)}, bf16[4,2,64,128]{3,2,1,0:T(8,128)(2,1)S(1)}, u32[]{:S(2)}, u32[]{:S(2)}) collective-permute-start(bf16[4,2,64,128]{3,2,1,0:T(8,128)(2,1)S(1)} %get-tuple-element.13), channel_id=1, source_target_pairs={{0,6},{2,4},{4,2},{6,0},{8,14},{10,12},{12,10},{14,8},{16,22},{18,... | collective-permute-start | bytes 393224 | tf_op jit(solution)/shard_map/ppermute | solution.py:27
  22.4 5.9 %collective-permute-start.5 = (bf16[4,2,64,128]{3,2,1,0:T(8,128)(2,1)S(1)}, bf16[4,2,64,128]{3,2,1,0:T(8,128)(2,1)S(1)}, u32[]{:S(2)}, u32[]{:S(2)}) collective-permute-start(bf16[4,2,64,128]{3,2,1,0:T(8,128)(2,1)S(1)} %get-tuple-element.13), channel_id=1, source_target_pairs={{0,4},{2,6},{4,0},{6,2},{8,12},{10,14},{12,8},{14,10},{16,20},{18,... | collective-permute-start | bytes 393224 | tf_op jit(solution)/shard_map/ppermute | solution.py:27
  22.9 5.5 %collective-permute-start.4 = (bf16[4,2,64,128]{3,2,1,0:T(8,128)(2,1)S(1)}, bf16[4,2,64,128]{3,2,1,0:T(8,128)(2,1)S(1)}, u32[]{:S(2)}, u32[]{:S(2)}) collective-permute-start(bf16[4,2,64,128]{3,2,1,0:T(8,128)(2,1)S(1)} %get-tuple-element.13), channel_id=1, source_target_pairs={{0,2},{2,0},{4,6},{6,4},{8,10},{10,8},{12,14},{14,12},{16,18},{18,... | collective-permute-start | bytes 393224 | tf_op jit(solution)/shard_map/ppermute | solution.py:27
  28.5 2.0 %collective-permute-start.7 = (bf16[16,2,64,128]{3,2,1,0:T(8,128)(2,1)S(1)}, bf16[16,2,64,128]{3,2,1,0:T(8,128)(2,1)S(1)}, u32[]{:S(2)}, u32[]{:S(2)}) collective-permute-start(bf16[16,2,64,128]{3,2,1,0:T(8,128)(2,1)S(1)} %bitcast.35), channel_id=1, source_target_pairs={{0,1},{1,0},{2,3},{3,2},{4,5},{5,4},{6,7},{7,6},{8,9},{9,8},{10,11... | collective-permute-start | bytes 1572872 | tf_op jit(solution)/shard_map/ppermute | solution.py:31
  30.5 1.2 %copy-start.7 = (bf16[32,128,128]{2,1,0:T(8,128)(2,1)S(1)}, bf16[32,128,128]{2,1,0:T(8,128)(2,1)}, u32[]{:S(2)}) copy-start(bf16[32,128,128]{2,1,0:T(8,128)(2,1)} %copy-done.6) | copy-start | bytes 3145732
  38.6 11.2 %collective-permute-start.10 = (f32[4,8,128]{1,2,0:T(8,128)S(1)}, f32[4,8,128]{1,2,0:T(8,128)S(1)}, u32[]{:S(2)}, u32[]{:S(2)}) collective-permute-start(f32[4,8,128]{1,2,0:T(8,128)S(1)} %bitcast.40), channel_id=1, source_target_pairs={{0,24},{2,26},{4,28},{6,30},{8,16},{10,18},{12,20},{14,22},{16,8},... | collective-permute-start | bytes 49160 | tf_op jit(solution)/shard_map/ppermute | solution.py:27
  40.8 23.1 %collective-permute-start.9 = (f32[4,8,128]{1,2,0:T(8,128)S(1)}, f32[4,8,128]{1,2,0:T(8,128)S(1)}, u32[]{:S(2)}, u32[]{:S(2)}) collective-permute-start(f32[4,8,128]{1,2,0:T(8,128)S(1)} %bitcast.41), channel_id=1, source_target_pairs={{0,16},{2,18},{4,20},{6,22},{8,24},{10,26},{12,28},{14,30},{16,0},... | collective-permute-start | bytes 49160 | tf_op jit(solution)/shard_map/ppermute | solution.py:27
  41.1 22.9 %collective-permute-start.8 = (f32[4,8,128]{1,2,0:T(8,128)S(1)}, f32[4,8,128]{1,2,0:T(8,128)S(1)}, u32[]{:S(2)}, u32[]{:S(2)}) collective-permute-start(f32[4,8,128]{1,2,0:T(8,128)S(1)} %bitcast.42), channel_id=1, source_target_pairs={{0,8},{2,10},{4,12},{6,14},{8,0},{10,2},{12,4},{14,6},{16,24},{18,... | collective-permute-start | bytes 49160 | tf_op jit(solution)/shard_map/ppermute | solution.py:27
  64.0 5.9 %collective-permute-start.13 = (f32[1,8,128]{1,2,0:T(8,128)S(1)}, f32[1,8,128]{1,2,0:T(8,128)S(1)}, u32[]{:S(2)}, u32[]{:S(2)}) collective-permute-start(f32[1,8,128]{1,2,0:T(8,128)S(1)} %get-tuple-element.10), channel_id=1, source_target_pairs={{0,6},{2,4},{4,2},{6,0},{8,14},{10,12},{12,10},{14,8},{16,22},{18,... | collective-permute-start | bytes 12296 | tf_op jit(solution)/shard_map/ppermute | solution.py:27
  65.7 4.6 %collective-permute-start.12 = (f32[1,8,128]{1,2,0:T(8,128)S(1)}, f32[1,8,128]{1,2,0:T(8,128)S(1)}, u32[]{:S(2)}, u32[]{:S(2)}) collective-permute-start(f32[1,8,128]{1,2,0:T(8,128)S(1)} %get-tuple-element.11), channel_id=1, source_target_pairs={{0,4},{2,6},{4,0},{6,2},{8,12},{10,14},{12,8},{14,10},{16,20},{18,... | collective-permute-start | bytes 12296 | tf_op jit(solution)/shard_map/ppermute | solution.py:27
  67.0 4.3 %collective-permute-start.11 = (f32[1,8,128]{1,2,0:T(8,128)S(1)}, f32[1,8,128]{1,2,0:T(8,128)S(1)}, u32[]{:S(2)}, u32[]{:S(2)}) collective-permute-start(f32[1,8,128]{1,2,0:T(8,128)S(1)} %get-tuple-element.9), channel_id=1, source_target_pairs={{0,2},{2,0},{4,6},{6,4},{8,10},{10,8},{12,14},{14,12},{16,18},{18,... | collective-permute-start | bytes 12296 | tf_op jit(solution)/shard_map/ppermute | solution.py:27
  71.3 1.2 %collective-permute-start.14 = (f32[8,16]{0,1:T(8,128)S(1)}, f32[8,16]{0,1:T(8,128)S(1)}, u32[]{:S(2)}, u32[]{:S(2)}) collective-permute-start(f32[8,16]{0,1:T(8,128)S(1)} %slice.21), channel_id=1, source_target_pairs={{0,1},{1,0},{2,3},{3,2},{4,5},{5,4},{6,7},{7,6},{8,9},{9,8},{10,11... | collective-permute-start | bytes 1544 | tf_op jit(solution)/shard_map/ppermute | solution.py:31
